TPU v7x, 128 devices: a whole 4x4x4 slice. The times are simulated.
128 devices in a mesh: section: 2 (over z_hi), render: 4 (over z_lo, core), dp: 16 (over y, x).
Axes of the slice: x: 4, y: 4, z: 4 (z_hi: 2, z_lo: 2; z = z_hi * 2 + z_lo), core: 2. Of those that a mesh axis runs over, the one named last changes fastest.
Arguments:
- section_tokens: bfloat16 [2, 16, 512, 2048], P('section', 'dp', 'render'), may hold values from -60 to 60
- w_qkv: bfloat16 [2, 2048, 3072], P('section', 'dp'), may hold values from -0.5 to 0.5
- w_out: bfloat16 [2, 1024, 2048], P('section', 'dp'), may hold values from -0.1875 to 0.1875
- gains: float32 [2, 2048], P('section'), may hold values from 0.25 to 1.75
- cotangent: bfloat16 [16, 512, 2048], P('dp', 'render'), may hold values from -6 to 6
Outputs:
- token_grads: bfloat16 [2, 16, 512, 2048], P('section', 'dp', 'render')
- qkv_grads: float32 [2, 2048, 3072], P('section', 'dp')
- out_grads: float32 [2, 1024, 2048], P('section', 'dp')
- gain_grads: float32 [2, 2048], P('section')
All inputs are finite; a program needn't handle non-finite values.
Results may differ from a plain program's by a relative error of at most 0.02.
Values may be sent and summed in bfloat16 or wider, within the bound.
No kernel may reach another device: no remote copies, remote signals or barrier semaphores. Data moves between devices by JAX's collectives and lax.ppermute only.
A program may use at most 192 MiB of HBM per device.

v0:
```python
import jax
import jax.numpy as jnp
from jax import lax
from jax.sharding import PartitionSpec as P

HEADS = 8
HD = 128
NORM_EPSILON = 1e-06


def joined_along(blocks, dim):
    blocks = jnp.moveaxis(blocks, 0, dim)
    lengths = blocks.shape
    return blocks.reshape(*lengths[:dim], lengths[dim] * lengths[dim + 1], *lengths[dim + 2 :])


def sent_to_all(shard, axis):
    peers = lax.axis_size(axis)
    return lax.all_to_all(
        jnp.broadcast_to(shard[None], (peers, *shard.shape)), axis, 0, 0, tiled=True
    )


def gather_directly(shard, axis, dim):
    return joined_along(sent_to_all(shard, axis), dim)


def shifted(block, axis, distance):
    devices = range(lax.axis_size(axis))
    route = [(i - distance, i) for i in devices if i - distance in devices]
    return lax.ppermute(block, axis, route)


def split_up(shard, dim, peers):
    lengths = shard.shape
    blocks = shard.reshape(*lengths[:dim], peers, lengths[dim] // peers, *lengths[dim + 1 :])
    return jnp.moveaxis(blocks, dim, 0)


def sum_at_owner(shard, axis, dim):
    blocks = split_up(shard, dim, lax.axis_size(axis))
    arrived = lax.all_to_all(blocks, axis, split_axis=0, concat_axis=0, tiled=True)
    return arrived.astype(jnp.float32).sum(axis=0)


def sent_together(arrays, axis, dim, along):
    widths = [a.shape[along] for a in arrays]
    both = jnp.concatenate(arrays, axis=along)
    out = lax.all_gather(both, axis, axis=dim, tiled=True)
    return tuple(jnp.split(out, [sum(widths[:k]) for k in range(1, len(widths))], axis=along))


def sum_packed(arrays, axis, dims):
    peers = lax.axis_size(axis)
    blocks = [split_up(a, dim, peers) for a, dim in zip(arrays, dims)]
    lines = jnp.concatenate([b.reshape(peers, -1) for b in blocks], axis=1)
    span = max(16, -(-lines.shape[1] // 1024) * 8)
    lines = jnp.pad(lines, ((0, 0), (0, span * 128 - lines.shape[1]))).reshape(-1, 128)
    line, at, finished = (lax.psum_scatter(lines, axis, tiled=True).reshape(-1), 0, [])
    for b in blocks:
        part = b[0]
        finished.append(line[at : at + part.size].reshape(part.shape))
        at += part.size
    return tuple(finished)


def gather_packed(arrays, axis, dims):
    line = jnp.concatenate([a.reshape(-1) for a in arrays])
    lines, at, finished = (lax.all_gather(line, axis), 0, [])
    for a, dim in zip(arrays, dims):
        blocks = lines[:, at : at + a.size].reshape(-1, *a.shape)
        finished.append(joined_along(blocks, dim))
        at += a.size
    return tuple(finished)


def over_copies(shard, axis):
    return sent_to_all(shard, axis).sum(axis=0)


def rms_norm(values, gain_row):
    wide_rows = values.astype(jnp.float32)
    row_scale = lax.rsqrt(jnp.mean(wide_rows * wide_rows, axis=-1, keepdims=True) + NORM_EPSILON)
    return ((wide_rows * row_scale * gain_row).astype(jnp.bfloat16), row_scale)


def norm_back(values, row_scale, gain_row, upstream):
    wide_rows = values.astype(jnp.float32)
    grad_wide = upstream.astype(jnp.float32)
    scaled = grad_wide * gain_row
    inner_sum = jnp.sum(scaled * wide_rows, axis=-1, keepdims=True)
    result = row_scale * scaled - wide_rows * row_scale**3 * inner_sum / values.shape[-1]
    gain_term = jnp.sum(grad_wide * wide_rows * row_scale, axis=0)
    return (result, gain_term)


def split_heads(values):
    return values.reshape(values.shape[0], HEADS, HD)


def only_when(flag, compute):

    def skipped():
        return jax.tree.map(jnp.zeros_like, compute())

    return lax.cond(flag, compute, skipped)


def attend(queries, key_rows, value_rows):
    factor = HD ** (-0.5)
    scores = (
        jnp.einsum(
            "qhd,khd->hqk",
            split_heads(queries),
            split_heads(key_rows),
            preferred_element_type=jnp.float32,
        )
        * factor
    )
    row_top = jnp.max(scores, axis=-1, keepdims=True)
    raised = jnp.exp(scores - row_top)
    row_total = jnp.sum(raised, axis=-1, keepdims=True)
    attn_prob = raised / row_total
    mixed_heads = jnp.einsum(
        "hqk,khd->qhd",
        attn_prob.astype(jnp.bfloat16),
        split_heads(value_rows),
        preferred_element_type=jnp.float32,
    )
    return (
        mixed_heads.reshape(queries.shape[0], HEADS * HD).astype(jnp.bfloat16),
        attn_prob,
        row_top,
        row_total,
    )


def score_grad(attn_prob, upstream, value_rows):
    factor = HD ** (-0.5)
    grad_prob = jnp.einsum(
        "qhd,khd->hqk",
        split_heads(upstream),
        split_heads(value_rows),
        preferred_element_type=jnp.float32,
    )
    row_delta = jnp.sum(grad_prob * attn_prob, axis=-1, keepdims=True)
    grad_score = (attn_prob * (grad_prob - row_delta) * factor).astype(jnp.bfloat16)
    return (grad_score, row_delta)


def key_terms_of(grad_score, attn_prob, queries, upstream):
    grad_key = jnp.einsum(
        "hqk,qhd->khd", grad_score, split_heads(queries), preferred_element_type=jnp.float32
    )
    grad_value = jnp.einsum(
        "hqk,qhd->khd",
        attn_prob.astype(jnp.bfloat16),
        split_heads(upstream),
        preferred_element_type=jnp.float32,
    )
    key_count = grad_key.shape[0]
    return (grad_key.reshape(key_count, HEADS * HD), grad_value.reshape(key_count, HEADS * HD))


def key_side(queries, upstream, row_top, row_total, row_delta, key_rows, value_rows):
    factor = HD ** (-0.5)
    scores = (
        jnp.einsum(
            "qhd,khd->hqk",
            split_heads(queries),
            split_heads(key_rows),
            preferred_element_type=jnp.float32,
        )
        * factor
    )
    attn_prob = jnp.exp(scores - row_top) / row_total
    grad_prob = jnp.einsum(
        "qhd,khd->hqk",
        split_heads(upstream),
        split_heads(value_rows),
        preferred_element_type=jnp.float32,
    )
    grad_score = (attn_prob * (grad_prob - row_delta) * factor).astype(jnp.bfloat16)
    grad_key, grad_value = key_terms_of(grad_score, attn_prob, queries, upstream)
    return jnp.concatenate([grad_key, grad_value], 1).astype(jnp.bfloat16)


def shards(section_tokens, w_qkv, w_out, gains, cotangent):
    tokens = section_tokens[0, 0]
    upstream = cotangent[0]
    gain_row = gains[0]
    head_width = HEADS * HD
    half_rows = tokens.shape[0] // 2
    section_index = lax.axis_index("section")
    is_encoder = section_index == 0
    is_decoder = jnp.logical_not(is_encoder)
    full_qkv, full_out = (
        lax.all_gather(w_qkv[0], "dp", axis=0, tiled=True),
        lax.all_gather(w_out[0], "dp", axis=0, tiled=True),
    )
    normed, row_scale = rms_norm(tokens, gain_row)
    projected = jnp.dot(normed, full_qkv, preferred_element_type=jnp.float32).astype(jnp.bfloat16)
    own_kv = projected[:, head_width:]
    enc_query = projected[half_rows:, :head_width]
    all_kv = gather_directly(own_kv, "render", 0)

    def encoder_forward():
        enc_mixed, enc_prob, enc_top, enc_total = attend(
            enc_query, all_kv[:, :head_width], all_kv[:, head_width:]
        )
        latent = (
            tokens[half_rows:].astype(jnp.float32)
            + jnp.dot(enc_mixed, full_out, preferred_element_type=jnp.float32)
        ).astype(jnp.bfloat16)
        return (enc_mixed, enc_prob, enc_top, enc_total, latent)

    enc_mixed, enc_prob, enc_top, enc_total, latent = only_when(is_encoder, encoder_forward)
    arrived = shifted(latent, "section", 1)

    def latent_project():
        lat_norm, lat_scale = rms_norm(arrived, gain_row)
        lat_kv = jnp.dot(
            lat_norm, full_qkv[:, head_width:], preferred_element_type=jnp.float32
        ).astype(jnp.bfloat16)
        return (lat_norm, lat_scale, lat_kv)

    lat_norm, lat_scale, lat_kv = only_when(is_decoder, latent_project)
    scene_kv = gather_directly(lat_kv, "render", 0)
    lat_count = scene_kv.shape[0]

    def decoder_attention():
        key_rows = jnp.concatenate(
            [scene_kv[:, :head_width], projected[:, head_width : 2 * head_width]], 0
        )
        value_rows = jnp.concatenate([scene_kv[:, head_width:], projected[:, 2 * head_width :]], 0)
        dec_query = projected[:, :head_width]
        dec_mixed, dec_prob, dec_top, dec_total = attend(dec_query, key_rows, value_rows)
        dec_out_part = jnp.einsum(
            "nc,nd->cd", dec_mixed, upstream, preferred_element_type=jnp.float32
        ).astype(jnp.bfloat16)
        grad_mixed = jnp.einsum(
            "nd,cd->nc", upstream, full_out, preferred_element_type=jnp.float32
        ).astype(jnp.bfloat16)
        dec_score, dec_delta = score_grad(dec_prob, grad_mixed, value_rows)
        dec_grad_query = jnp.einsum(
            "hqk,khd->qhd", dec_score, split_heads(key_rows), preferred_element_type=jnp.float32
        ).reshape(dec_query.shape[0], head_width)
        dec_grad_key, dec_grad_value = key_terms_of(dec_score, dec_prob, dec_query, grad_mixed)
        lat_terms = jnp.concatenate([dec_grad_key[:lat_count], dec_grad_value[:lat_count]], 1)
        dec_grad_proj = jnp.concatenate(
            [dec_grad_query, dec_grad_key[lat_count:], dec_grad_value[lat_count:]], 1
        ).astype(jnp.bfloat16)
        return (lat_terms, dec_grad_proj, dec_out_part)

    lat_terms, dec_grad_proj, dec_out_part = only_when(is_decoder, decoder_attention)
    lat_grad = sum_at_owner(lat_terms.astype(jnp.bfloat16), "render", 0).astype(jnp.bfloat16)

    def decoder_finish():
        dec_qkv_part = jnp.einsum(
            "nd,nc->dc", normed, dec_grad_proj, preferred_element_type=jnp.float32
        )
        lat_weight_part = jnp.einsum(
            "nd,nc->dc", lat_norm, lat_grad, preferred_element_type=jnp.float32
        )
        dec_qkv_part = dec_qkv_part.at[:, head_width:].add(lat_weight_part).astype(jnp.bfloat16)
        grad_normed = jnp.einsum(
            "nc,dc->nd", dec_grad_proj, full_qkv, preferred_element_type=jnp.float32
        ).astype(jnp.bfloat16)
        grad_lat_norm = jnp.einsum(
            "nc,dc->nd", lat_grad, full_qkv[:, head_width:], preferred_element_type=jnp.float32
        ).astype(jnp.bfloat16)
        dec_back, dec_gain_first = norm_back(tokens, row_scale, gain_row, grad_normed)
        dec_result = (upstream.astype(jnp.float32) + dec_back).astype(jnp.bfloat16)
        lat_back, dec_gain_second = norm_back(arrived, lat_scale, gain_row, grad_lat_norm)
        return (
            dec_qkv_part,
            dec_result,
            lat_back.astype(jnp.bfloat16),
            dec_gain_first + dec_gain_second,
        )

    dec_qkv_part, dec_result, lat_back, dec_gain = only_when(is_decoder, decoder_finish)
    returned = shifted(lat_back, "section", -1)

    def encoder_back_queries():
        enc_values = all_kv[:, head_width:]
        enc_keys = all_kv[:, :head_width]
        enc_out_part = jnp.einsum(
            "nc,nd->cd", enc_mixed, returned, preferred_element_type=jnp.float32
        ).astype(jnp.bfloat16)
        grad_enc_mixed = jnp.einsum(
            "nd,cd->nc", returned, full_out, preferred_element_type=jnp.float32
        ).astype(jnp.bfloat16)
        enc_score, enc_delta = score_grad(enc_prob, grad_enc_mixed, enc_values)
        query_grad = (
            jnp.einsum(
                "hqk,khd->qhd", enc_score, split_heads(enc_keys), preferred_element_type=jnp.float32
            )
            .reshape(half_rows, head_width)
            .astype(jnp.bfloat16)
        )
        return (enc_out_part, grad_enc_mixed, enc_delta, query_grad)

    enc_out_part, grad_enc_mixed, enc_delta, query_grad = only_when(
        is_encoder, encoder_back_queries
    )
    all_query, all_upstream = sent_together((enc_query, grad_enc_mixed), "render", 0, 1)
    all_top, all_total, all_delta = sent_together((enc_top, enc_total, enc_delta), "render", 1, 0)

    def own_key_grads():
        return key_side(
            all_query,
            all_upstream,
            all_top,
            all_total,
            all_delta,
            own_kv[:, :head_width],
            own_kv[:, head_width:],
        )

    key_grad = only_when(is_encoder, own_key_grads)

    def encoder_finish():
        query_weight_part = jnp.einsum(
            "nd,nc->dc", normed[half_rows:], query_grad, preferred_element_type=jnp.float32
        )
        key_weight_part = jnp.einsum(
            "nd,nc->dc", normed, key_grad, preferred_element_type=jnp.float32
        )
        enc_qkv_part = jnp.concatenate([query_weight_part, key_weight_part], 1).astype(jnp.bfloat16)
        grad_enc_norm = jnp.einsum(
            "nc,dc->nd", key_grad, full_qkv[:, head_width:], preferred_element_type=jnp.float32
        )
        query_back = jnp.einsum(
            "nc,dc->nd", query_grad, full_qkv[:, :head_width], preferred_element_type=jnp.float32
        )
        grad_enc_norm = grad_enc_norm.at[half_rows:].add(query_back).astype(jnp.bfloat16)
        enc_back, enc_gain_term = norm_back(tokens, row_scale, gain_row, grad_enc_norm)
        enc_result = enc_back.at[half_rows:].add(returned.astype(jnp.float32)).astype(jnp.bfloat16)
        return (enc_qkv_part, enc_result, enc_gain_term)

    enc_qkv_part, enc_result, enc_gain_term = only_when(is_encoder, encoder_finish)
    token_grad = jnp.where(is_encoder, enc_result, dec_result)
    qkv_part = jnp.where(is_encoder, enc_qkv_part, dec_qkv_part).astype(jnp.float32)
    out_part = jnp.where(is_encoder, enc_out_part, dec_out_part).astype(jnp.float32)
    gain_part = jnp.where(is_encoder, enc_gain_term, dec_gain)
    qkv_total, out_total = (
        lax.psum_scatter(
            qkv_part.astype(jnp.bfloat16), "render", scatter_dimension=1, tiled=True
        ).astype(jnp.float32),
        lax.psum_scatter(
            out_part.astype(jnp.bfloat16), "render", scatter_dimension=1, tiled=True
        ).astype(jnp.float32),
    )
    qkv_total, out_total = tuple(
        (
            part.astype(jnp.float32)
            for part in sum_packed(
                (qkv_total.astype(jnp.bfloat16), out_total.astype(jnp.bfloat16)), "dp", (0, 0)
            )
        )
    )
    qkv_total, out_total = tuple(
        (
            part.astype(jnp.float32)
            for part in gather_packed(
                (qkv_total.astype(jnp.bfloat16), out_total.astype(jnp.bfloat16)), "render", (1, 1)
            )
        )
    )
    gain_total = over_copies(gain_part, ("render", "dp"))
    return (token_grad[None, None], qkv_total[None], out_total[None], gain_total[None])


def solution(mesh):
    in_specs = (
        P("section", "dp", "render", None),
        P("section", "dp", None),
        P("section", "dp", None),
        P("section", None),
        P("dp", "render", None),
    )
    out_specs = (
        P("section", "dp", "render", None),
        P("section", "dp", None),
        P("section", "dp", None),
        P("section", None),
    )
    return jax.shard_map(shards, mesh=mesh, in_specs=in_specs, out_specs=out_specs, check_vma=False)
```

profile of v0, /device:TPU:1, one launch (start us, length us, event | category | flops | bytes accessed | tf_op | source)
XLA Modules:
  0.0 694.2 jit_solution(12119105009085443958)
XLA Ops:
  11.1 92.1 %all-gather.10.cloned.1.call-done = bf16[1,2048,3072]{2,1,0:T(8,128)(2,1)} async-done(((bf16[1,128,3072]{2,1,0:T(8,128)(2,1)}), bf16[1,2048,3072]{2,1,0:T(8,128)(2,1)}) %all-gather.10.cloned.1.call-update) | async-done | bytes 12582928 | tf_op jit(solution)/shard_map/all_gather | solution.py:198
  103.3 6.4 convolution_convert_fusion.11
  111.6 5.1 all-to-all-start
  117.4 24.3 %all-to-all-done = bf16[4,128,2048]{1,2,0:T(8,128)(2,1)} async-done(((bf16[4,128,2048]{1,2,0:T(8,128)(2,1)}), bf16[4,128,2048]{1,2,0:T(8,128)(2,1)}, u32[]{:S(2)}, u32[]{:S(2)}) %all-to-all-start) | async-done | bytes 2097184 | tf_op jit(solution)/shard_map/all_to_all | solution.py:19
  141.6 2.9 copy.319
  144.6 12.0 %all-gather.12.cloned.1.call-done = bf16[1,1024,2048]{2,1,0:T(8,128)(2,1)} async-done(((bf16[1,64,2048]{2,1,0:T(8,128)(2,1)}), bf16[1,1024,2048]{2,1,0:T(8,128)(2,1)}) %all-gather.12.cloned.1.call-update) | async-done | bytes 4194320 | tf_op jit(solution)/shard_map/all_gather | solution.py:199
  156.5 13.9 %conditional.7 = (bf16[64,1024]{1,0:T(8,128)(2,1)}, f32[8,64,512]{2,1,0:T(8,128)}, f32[8,64,1]{1,0,2:T(8,128)}, f32[8,64,1]{1,0,2:T(8,128)}, bf16[64,2048]{1,0:T(8,128)(2,1)S(1)}) conditional(s32[]{:T(128)} %convert_element_type.206, () %tuple.79, (bf16[64,1024]{1,0:T(8,128)(2,1)}, bf16[512,2048]{1,0:T(8,128)(2,1)S(1)}, ...), branch_computations={%region_1.0_spmd, %region_2.0_spmd} | conditional | flops 404945920 | bytes 37890116 | solution.py:106
  156.5 2.5 copy.320
  164.4 2.0 fusion.2
  172.5 5.6 collective-permute-done
  179.9 5.4 all-to-all-start.1
  185.4 13.7 %all-to-all-done.1 = bf16[4,64,2048]{2,1,0:T(8,128)(2,1)} async-done(((bf16[4,64,2048]{2,1,0:T(8,128)(2,1)}), bf16[4,64,2048]{2,1,0:T(8,128)(2,1)}, u32[]{:S(2)}, u32[]{:S(2)}) %all-to-all-start.1) | async-done | bytes 1048608 | tf_op jit(solution)/shard_map/all_to_all | solution.py:19
  199.1 5.0 conditional.9
  201.1 2.5 broadcast.186
  204.1 2.3 copy.321
  206.4 5.1 all-to-all-start.2
  211.5 13.7 %all-to-all-done.2 = bf16[4,64,2048]{2,1,0:T(8,128)(2,1)} async-done(((bf16[4,64,2048]{2,1,0:T(8,128)(2,1)}), bf16[4,64,2048]{2,1,0:T(8,128)(2,1)}, u32[]{:S(2)}, u32[]{:S(2)}) %all-to-all-start.2) | async-done | bytes 1048608 | tf_op jit(solution)/shard_map/all_to_all | solution.py:42
  225.2 7.8 %conditional.10 = (bf16[128,2048]{1,0:T(8,128)(2,1)}, bf16[64,2048]{1,0:T(8,128)(2,1)}, f32[2048]{0:T(1024)S(1)}, bf16[2048,3072]{0,1:T(8,128)(2,1)}) conditional(s32[]{:T(128)} %convert_element_type.210, () %tuple.81, (bf16[128,2048]{1,0:T(8,128)(2,1)S(1)}, bf16[128,3072]{0,1:T(8,128)(2,1)}, bf16[4,64,2048]{2,1,0:T(8,128)(2,1)}, ...), branch_computations={%region_13.0_spmd, %region_14.20_spmd} | conditional | flops 4313053184 | bytes 156054880 | solution.py:106
  226.8 6.1 broadcast.189.clone
  234.3 124.3 %collective-permute-done.1 = bf16[64,2048]{1,0:T(8,128)(2,1)S(1)} collective-permute-done((bf16[64,2048]{1,0:T(8,128)(2,1)}, bf16[64,2048]{1,0:T(8,128)(2,1)S(1)}, u32[]{:S(2)}, u32[]{:S(2)}) %collective-permute-start.1) | collective-permute-done | bytes 262176 | tf_op jit(solution)/shard_map/ppermute | solution.py:31
  358.7 15.2 %conditional.11 = (bf16[1024,2048]{1,0:T(8,128)(2,1)}, bf16[64,1024]{1,0:T(8,128)(2,1)S(1)}, f32[8,64,1]{1,0,2:T(8,128)}, bf16[64,1024]{1,0:T(8,128)(2,1)S(1)}) conditional(s32[]{:T(128)} %convert_element_type.206, () %tuple.78, (bf16[64,1024]{1,0:T(8,128)(2,1)}, bf16[64,2048]{1,0:T(8,128)(2,1)S(1)}, bf16[1024,2048]{1,0:T(8,128)(2,1)}, ...), branch_computations={%region_20.21_spmd, %region_21.23_spmd} | conditional | flops 674889216 | bytes 42209396 | solution.py:106
  358.9 2.5 copy.323
  365.6 2.3 multiply_reduce_fusion.1
  369.7 4.2 convolution_convert_fusion.5
  375.5 4.7 broadcast_select_fusion.1
  381.1 7.2 %all_gather.21 = f32[24,256,1]{0,2,1:T(1,128)S(1)} all-gather(f32[24,64,1]{0,2,1:T(1,128)S(1)} %copy.324), channel_id=1, replica_groups=mesh['section'=2,'render'=4,'dp'=16] {'render'}, dimensions={1}, use_global_device_ids=true | all-gather | bytes 30720 | tf_op jit(solution)/shard_map/all_gather | solution.py:49
  388.3 6.6 all-gather.8.cloned.1.call-done
  394.9 8.9 %conditional.12 = (bf16[128,2048]{0,1:T(8,128)(2,1)S(1)}) conditional(s32[]{:T(128)} %convert_element_type.206, () %tuple.88, (bf16[256,2048]{1,0:T(8,128)(2,1)}, bf16[128,2048]{1,0:T(8,128)(2,1)S(1)}, f32[24,256,1]{0,2,1:T(1,128)S(1)}) %tuple.191), branch_computations={%region_23.24_spmd, %region_24.0_spmd} | conditional | flops 271843328 | bytes 13754376 | solution.py:106
  398.3 1.9 fusion.93
  400.2 2.3 fusion.96
  403.8 32.5 %conditional.13 = (bf16[2048,3072]{0,1:T(8,128)(2,1)}, bf16[128,2048]{1,0:T(8,128)(2,1)}, f32[2048]{0:T(1024)S(1)}) conditional(s32[]{:T(128)} %convert_element_type.206, () %tuple.77, (bf16[128,2048]{1,0:T(8,128)(2,1)S(1)}, bf16[64,1024]{1,0:T(8,128)(2,1)S(1)}, bf16[128,2048]{0,1:T(8,128)(2,1)S(1)}, f32[128,1]{0,1:T(1,128)}, ...), branch_computations={%region_25.0_spmd, %region_26.29_spmd} | conditional | flops 2721184000 | bytes 65828460 | solution.py:106
  405.5 7.2 %fusion.101 = f32[128,2048]{1,0:T(8,128)S(1)} fusion(bf16[128,2048]{0,1:T(8,128)(2,1)} %copy-done.8, bf16[2048,3072]{1,0:T(8,128)(2,1)} %get-tuple-element.182), kind=kOutput, calls=%fused_computation.122 | convolution fusion | flops 1073741824 | bytes 9961472 | tf_op jit(solution)/shard_map/cond/branch_1_fun/nc,dc->nd/dot_general | solution.py:331
  412.7 3.6 fusion.108
  419.4 2.3 convolution_convert_fusion.9
  421.7 14.6 %pad_maximum_fusion.5 = bf16[2048,3072]{0,1:T(8,128)(2,1)} fusion(bf16[2048,2048]{0,1:T(8,128)(2,1)S(1)} %convolution_convert_fusion.9, bf16[2048,1024]{0,1:T(8,128)(2,1)S(1)} %convolution_convert_fusion.10), kind=kLoop, calls=%fused_computation.121 | loop fusion | flops 25165824 | bytes 25165824 | tf_op jit(solution)/shard_map/cond/branch_1_fun/concatenate | solution.py:330
  436.3 10.7 %broadcast_select_fusion = bf16[2048,3072]{0,1:T(8,128)(2,1)} fusion(bf16[2048,3072]{0,1:T(8,128)(2,1)} %get-tuple-element.228, bf16[2048,3072]{0,1:T(8,128)(2,1)} %get-tuple-element.472, pred[]{:T(512)S(6)} %eq.3), kind=kLoop, calls=%fused_computation.146 | loop fusion | flops 6291456 | bytes 37748736 | tf_op jit(solution)/shard_map/jit(_where)/select_n | solution.py:344
  447.3 2.3 reshape_reshape.7
  449.7 110.1 %reduce-scatter.4.cloned.1.call-done = bf16[2048,768]{0,1:T(8,128)(2,1)} async-done(((bf16[2048,3072]{0,1:T(8,128)(2,1)}), bf16[2048,768]{0,1:T(8,128)(2,1)}) %reduce-scatter.4.cloned.1.call-update) | async-done | bytes 3145744 | tf_op jit(solution)/shard_map/reduce_scatter | solution.py:348
  559.8 3.2 copy.330
  563.0 2.6 reshape_reshape.6
  565.6 4.4 pad_maximum_fusion.6
  570.0 4.9 reshape.278
  574.9 76.6 %reduce-scatter.8.cloned.1.call-done = bf16[1024,128]{1,0:T(8,128)(2,1)} async-done(((bf16[16384,128]{1,0:T(8,128)(2,1)}), bf16[1024,128]{1,0:T(8,128)(2,1)}) %reduce-scatter.8.cloned.1.call-update) | async-done | bytes 262160 | tf_op jit(solution)/shard_map/reduce_scatter | solution.py:59
  655.2 8.7 %all-to-all-start.3 = ((f32[64,1,2048]{2,1,0:T(1,128)}), f32[64,1,2048]{2,1,0:T(1,128)S(1)}, u32[]{:S(2)}, u32[]{:S(2)}) async-start(f32[64,1,2048]{2,1,0:T(1,128)} %broadcast_in_dim.29), calls=%async_computation.6 | async-start | bytes 1048576 | tf_op jit(solution)/shard_map/all_to_all | solution.py:19
  663.9 1.9 select_bitcast_fusion
  665.8 10.2 %all-to-all-done.3 = f32[64,1,2048]{2,1,0:T(1,128)S(1)} async-done(((f32[64,1,2048]{2,1,0:T(1,128)}), f32[64,1,2048]{2,1,0:T(1,128)S(1)}, u32[]{:S(2)}, u32[]{:S(2)}) %all-to-all-start.3) | async-done | bytes 524320 | tf_op jit(solution)/shard_map/all_to_all | solution.py:19
  677.0 4.5 all-gather.14.cloned.1.call-done
  684.9 2.0 reshape.281
  (105 shorter events, 51.4 us)
Async XLA Ops:
  7.2 96.1 %all-gather.10.cloned.1.call-start = ((), (), s32[]{:S(2)}) async-start(), calls=%async_computation.11 | async-start | bytes 13369344 | tf_op jit(solution)/shard_map/all_gather | solution.py:198
  7.9 148.6 %all-gather.12.cloned.1.call-start = ((), (), s32[]{:S(2)}) async-start(), calls=%async_computation.12 | async-start | bytes 4456448 | tf_op jit(solution)/shard_map/all_gather | solution.py:199
  9.9 215.3 %copy-start.19 = (f32[128,1]{0,1:T(1,128)}, f32[128,1]{0,1:T(1,128)S(1)}, u32[]{:S(2)}) copy-start(f32[128,1]{0,1:T(1,128)S(1)} %get-tuple-element.506) | copy-start | bytes 1540
  109.6 7.1 %copy-start.3 = (bf16[128,3072]{1,0:T(8,128)(2,1)}, bf16[128,3072]{1,0:T(8,128)(2,1)S(1)}, u32[]{:S(2)}) copy-start(bf16[128,3072]{1,0:T(8,128)(2,1)S(1)} %convolution_convert_fusion.11) | copy-start | bytes 2359300
  109.7 1.9 copy-start.6
  111.6 30.0 %all-to-all-start = ((bf16[4,128,2048]{1,2,0:T(8,128)(2,1)}), bf16[4,128,2048]{1,2,0:T(8,128)(2,1)}, u32[]{:S(2)}, u32[]{:S(2)}) async-start(bf16[4,128,2048]{1,2,0:T(8,128)(2,1)} %broadcast_in_dim.22), calls=%async_computation | async-start | bytes 4194304 | tf_op jit(solution)/shard_map/all_to_all | solution.py:19
  116.7 39.8 %copy-start.2 = (bf16[1,1,128,2048]{3,2,1,0:T(8,128)(2,1)S(1)}, bf16[1,1,128,2048]{3,2,1,0:T(8,128)(2,1)}, u32[]{:S(2)}) copy-start(bf16[1,1,128,2048]{3,2,1,0:T(8,128)(2,1)} %param.25) | copy-start | bytes 1572868
  156.5 21.5 %copy-start.14 = (f32[1,2048]{1,0:T(1,128)S(1)}, f32[1,2048]{1,0:T(1,128)}, u32[]{:S(2)}) copy-start(f32[1,2048]{1,0:T(1,128)} %param.28) | copy-start | bytes 24580
  162.6 6.1 copy-start
  170.5 0.7 copy-start.15
  171.2 6.9 collective-permute-start
  179.9 19.1 %all-to-all-start.1 = ((bf16[4,64,2048]{2,1,0:T(8,128)(2,1)}), bf16[4,64,2048]{2,1,0:T(8,128)(2,1)}, u32[]{:S(2)}, u32[]{:S(2)}) async-start(bf16[4,64,2048]{2,1,0:T(8,128)(2,1)} %broadcast_in_dim.25), calls=%async_computation.1 | async-start | bytes 2097152 | tf_op jit(solution)/shard_map/all_to_all | solution.py:19
  206.4 18.8 %all-to-all-start.2 = ((bf16[4,64,2048]{2,1,0:T(8,128)(2,1)}), bf16[4,64,2048]{2,1,0:T(8,128)(2,1)}, u32[]{:S(2)}, u32[]{:S(2)}) async-start(bf16[4,64,2048]{2,1,0:T(8,128)(2,1)} %bitcast.193), calls=%async_computation.2 | async-start | bytes 2097152 | tf_op jit(solution)/shard_map/all_to_all | solution.py:42
  211.5 183.4 %all-gather.8.cloned.1.call-start = ((), (), s32[]{:S(2)}) async-start(), calls=%async_computation.7 | async-start | bytes 1310720 | tf_op jit(solution)/shard_map/all_gather | solution.py:49
  233.0 125.6 %copy-start.17 = (f32[2048]{0:T(1024)}, f32[2048]{0:T(1024)S(1)}, u32[]{:S(2)}) copy-start(f32[2048]{0:T(1024)S(1)} %get-tuple-element.233) | copy-start | bytes 24580
  233.0 125.6 %collective-permute-start.1 = (bf16[64,2048]{1,0:T(8,128)(2,1)}, bf16[64,2048]{1,0:T(8,128)(2,1)S(1)}, u32[]{:S(2)}, u32[]{:S(2)}) collective-permute-start(bf16[64,2048]{1,0:T(8,128)(2,1)} %get-tuple-element.219), channel_id=1, source_target_pairs={{64,0},{65,1},{66,2},{67,3},{68,4},{69,5},{70,6},{71,7},{72,8},{73... | collective-permute-start | bytes 786440 | tf_op jit(solution)/shard_map/ppermute | solution.py:31
  361.4 2.8 copy-start.1
  365.6 4.0 copy-start.11
  369.6 4.2 copy-start.12
  375.5 71.9 %reduce-scatter.6.cloned.1.call-start = ((), (), s32[]{:S(2)}) async-start(), calls=%async_computation.9 | async-start | bytes 5242880 | tf_op jit(solution)/shard_map/reduce_scatter | solution.py:351
  380.2 14.7 %copy-start.7 = (bf16[128,2048]{1,0:T(8,128)(2,1)S(1)}, bf16[128,2048]{1,0:T(8,128)(2,1)}, u32[]{:S(2)}) copy-start(bf16[128,2048]{1,0:T(8,128)(2,1)} %copy-done.6) | copy-start | bytes 1572868
  380.2 179.5 %reduce-scatter.4.cloned.1.call-start = ((), (), s32[]{:S(2)}) async-start(), calls=%async_computation.8 | async-start | bytes 15728640 | tf_op jit(solution)/shard_map/reduce_scatter | solution.py:348
  404.1 0.8 copy-start.8
  412.7 3.6 copy-start.20
  418.0 1.3 copy-start.9
  447.0 204.6 %reduce-scatter.8.cloned.1.call-start = ((), (), s32[]{:S(2)}) async-start(), calls=%async_computation.10 | async-start | bytes 4456448 | tf_op jit(solution)/shard_map/reduce_scatter | solution.py:59
  574.9 79.2 %copy-start.18 = (f32[2048]{0:T(1024)S(1)}, f32[2048]{0:T(1024)}, u32[]{:S(2)}) copy-start(f32[2048]{0:T(1024)} %copy-done.17) | copy-start | bytes 24580
  574.9 106.6 %all-gather.14.cloned.1.call-start = ((), (), s32[]{:S(2)}) async-start(), calls=%async_computation.13 | async-start | bytes 1310720 | tf_op jit(solution)/shard_map/all_gather | solution.py:69
  655.2 20.8 %all-to-all-start.3 = ((f32[64,1,2048]{2,1,0:T(1,128)}), f32[64,1,2048]{2,1,0:T(1,128)S(1)}, u32[]{:S(2)}, u32[]{:S(2)}) async-start(f32[64,1,2048]{2,1,0:T(1,128)} %broadcast_in_dim.29), calls=%async_computation.6 | async-start | bytes 1048576 | tf_op jit(solution)/shard_map/all_to_all | solution.py:19
Sparse Core Ops, SparseCore 0:
  10.1 93.0 all-gather.9
  105.4 51.1 all-gather.11
  375.6 19.2 all-gather.7
  397.2 46.0 reduce-scatter.5
  447.1 112.6 reduce-scatter.3
  575.0 76.4 reduce-scatter.7
  654.2 27.2 all-gather.13
where the time goes:
time: 702 us; the launch traced here: 694 us
  waiting for transfers between devices  495 us (71%)
  local copies, waits for them, and re-layouts  58 us (8%)
  other arithmetic  50.1 us (7%)
  matrix products  40.3 us (6%)
  starting transfers between devices  27.4 us (4%)
  between operations  14.8 us (2%)
  blocking collectives  7.17 us (1%)
    ppermute x2, waiting for transfers between devices, shifted(): return lax.ppermute(block, axis, route)  130 us
    reduce_scatter x1, waiting for transfers between devices, shards(): lax.psum_scatter(qkv_part.astype(jnp.bfloat16), 'render', scatter_dimensi...  110 us
    all_gather x1, waiting for transfers between devices, shards(): lax.all_gather(w_qkv[0], 'dp', axis=0, tiled=True)  92.1 us
    reduce_scatter x1, waiting for transfers between devices, sum_packed(): lax.psum_scatter(lines, axis, tiled=True).reshape(-1)  76.6 us
    all_to_all x3, waiting for transfers between devices, sent_to_all(): lax.all_to_all(jnp.broadcast_to(shard[None], (peers, *shard.shape)), axis...  48.2 us
    another operation x15, local copies, waits for them, and re-layouts  19.8 us
    all_to_all x3, starting transfers between devices, sent_to_all(): lax.all_to_all(jnp.broadcast_to(shard[None], (peers, *shard.shape)), axis...  19.2 us
    concatenate x1, other arithmetic, encoder_finish(): jnp.concatenate([query_weight_part, key_weight_part], 1)  14.6 us
  transfers between devices with their start and end apart: 13, of which 12 were waited for; matrix products, arithmetic and copies ran while one was open for 11% of the time, Pallas kernels for 0%

commit v1 on v0

--- a/solution.py
+++ b/solution.py
@@ -6,6 +6,24 @@
 HEADS = 8
 HD = 128
 NORM_EPSILON = 1e-06
+
+
+def collect(array, axis, dim):
+    ways, here, step = (lax.axis_size(axis), lax.axis_index(axis), array.shape[dim])
+    lengths = [n * ways if d == dim else n for d, n in enumerate(array.shape)]
+    full = lax.dynamic_update_slice_in_dim(
+        jnp.zeros(lengths, array.dtype), array, here * step, axis=dim
+    )
+    going_up = going_down = array
+    for far in range(1, ways // 2 + 1):
+        going_up = lax.ppermute(going_up, axis, [(d, (d + 1) % ways) for d in range(ways)])
+        full = lax.dynamic_update_slice_in_dim(full, going_up, (here - far) % ways * step, axis=dim)
+        if 2 * far < ways:
+            going_down = lax.ppermute(going_down, axis, [(d, (d - 1) % ways) for d in range(ways)])
+            full = lax.dynamic_update_slice_in_dim(
+                full, going_down, (here + far) % ways * step, axis=dim
+            )
+    return full
 
 
 def joined_along(blocks, dim):
@@ -195,7 +213,7 @@
     is_encoder = section_index == 0
     is_decoder = jnp.logical_not(is_encoder)
     full_qkv, full_out = (
-        lax.all_gather(w_qkv[0], "dp", axis=0, tiled=True),
+        collect(w_qkv[0], "dp", 0),
         lax.all_gather(w_out[0], "dp", axis=0, tiled=True),
     )
     normed, row_scale = rms_norm(tokens, gain_row)

time: 702 us -> 775 us (1.10)
  starting transfers between devices: 27.4 us -> 77.5 us
  local copies, waits for them, and re-layouts: 58 us -> 84.9 us
    ppermute x0 -> x15, waiting for transfers between devices: none -> 104 us  [the longest x8 89 us: collect(): lax.ppermute(going_up, axis, [(d, (d + 1) % ways) for d in range(ways)])]
    all_gather x1 -> x0, waiting for transfers between devices: 92.1 us -> none  [shards(): lax.all_gather(w_qkv[0], 'dp', axis=0, tiled=True)]
    ppermute x0 -> x15, starting transfers between devices: none -> 36.9 us  [the longest x7 34.8 us: collect(): lax.ppermute(going_down, axis, [(d, (d - 1) % ways) for d in range(ways)])]
    dynamic_update_slice x0 -> x16, local copies, waits for them, and re-layouts: none -> 20.9 us  [the longest x8 11 us: collect(): lax.dynamic_update_slice_in_dim(full, going_up, (here - far) % ways * ste...]
    all_to_all x3, starting transfers between devices: 19.2 us -> 32.4 us  [sent_to_all(): lax.all_to_all(jnp.broadcast_to(shard[None], (peers, *shard.shape)), axis...]
    all_gather x1, waiting for transfers between devices: 12 us -> 0.02 us  [shards(): lax.all_gather(w_out[0], 'dp', axis=0, tiled=True)]
    another operation x15 -> x16, local copies, waits for them, and re-layouts: 19.8 us -> 25.9 us
  transfers between devices with their start and end apart: 13 -> 27, of which waited for: 12 -> 23; matrix products, arithmetic and copies ran while one was open for 11% -> 14% of each run, Pallas kernels for 0% -> 0%
where the time goes in v1:
time: 775 us; the launch traced here: 765 us
  waiting for transfers between devices  489 us (63%)
  local copies, waits for them, and re-layouts  84.9 us (11%)
  starting transfers between devices  77.5 us (10%)
  other arithmetic  49.3 us (6%)
  matrix products  41 us (5%)
  between operations  14.9 us (2%)
    ppermute x2, waiting for transfers between devices, shifted(): return lax.ppermute(block, axis, route)  130 us
    reduce_scatter x1, waiting for transfers between devices, shards(): lax.psum_scatter(qkv_part.astype(jnp.bfloat16), 'render', scatter_dimensi...  110 us
    ppermute x8, waiting for transfers between devices, collect(): lax.ppermute(going_up, axis, [(d, (d + 1) % ways) for d in range(ways)])  89 us
    reduce_scatter x1, waiting for transfers between devices, sum_packed(): lax.psum_scatter(lines, axis, tiled=True).reshape(-1)  76.7 us
    all_to_all x3, waiting for transfers between devices, sent_to_all(): lax.all_to_all(jnp.broadcast_to(shard[None], (peers, *shard.shape)), axis...  47.1 us
    ppermute x7, starting transfers between devices, collect(): lax.ppermute(going_down, axis, [(d, (d - 1) % ways) for d in range(ways)])  34.8 us
    all_to_all x3, starting transfers between devices, sent_to_all(): lax.all_to_all(jnp.broadcast_to(shard[None], (peers, *shard.shape)), axis...  32.4 us
    another operation x16, local copies, waits for them, and re-layouts  25.9 us
  transfers between devices with their start and end apart: 27, of which 23 were waited for; matrix products, arithmetic and copies ran while one was open for 14% of the time, Pallas kernels for 0%

profile of v1, /device:TPU:1, one launch (start us, length us, event | category | flops | bytes accessed | tf_op | source)
XLA Modules:
  0.0 764.8 jit_solution(290428028269016351)
XLA Ops:
  9.3 3.8 collective-permute-start.1
  13.1 17.3 %collective-permute-done = bf16[128,3072]{1,0:T(8,128)(2,1)S(1)} collective-permute-done((bf16[128,3072]{1,0:T(8,128)(2,1)}, bf16[128,3072]{1,0:T(8,128)(2,1)S(1)}, u32[]{:S(2)}, u32[]{:S(2)}) %collective-permute-start) | collective-permute-done | bytes 786464 | tf_op jit(solution)/shard_map/ppermute | solution.py:19
  32.0 4.6 collective-permute-start.3
  36.6 16.7 %collective-permute-done.2 = bf16[128,3072]{1,0:T(8,128)(2,1)S(1)} collective-permute-done((bf16[128,3072]{1,0:T(8,128)(2,1)S(1)}, bf16[128,3072]{1,0:T(8,128)(2,1)S(1)}, u32[]{:S(2)}, u32[]{:S(2)}) %collective-permute-start.2) | collective-permute-done | bytes 786464 | tf_op jit(solution)/shard_map/ppermute | solution.py:19
  53.3 6.1 broadcast.217
  60.4 4.8 collective-permute-start.5
  65.1 8.9 %collective-permute-done.4 = bf16[128,3072]{1,0:T(8,128)(2,1)} collective-permute-done((bf16[128,3072]{1,0:T(8,128)(2,1)S(1)}, bf16[128,3072]{1,0:T(8,128)(2,1)}, u32[]{:S(2)}, u32[]{:S(2)}) %collective-permute-start.4) | collective-permute-done | bytes 786464 | tf_op jit(solution)/shard_map/ppermute | solution.py:19
  78.5 5.5 collective-permute-start.7
  84.9 16.2 %collective-permute-done.6 = bf16[128,3072]{1,0:T(8,128)(2,1)} collective-permute-done((bf16[128,3072]{1,0:T(8,128)(2,1)}, bf16[128,3072]{1,0:T(8,128)(2,1)}, u32[]{:S(2)}, u32[]{:S(2)}) %collective-permute-start.6) | collective-permute-done | bytes 786464 | tf_op jit(solution)/shard_map/ppermute | solution.py:19
  104.3 7.5 collective-permute-done.7
  111.8 5.4 collective-permute-start.9
  127.4 5.5 collective-permute-start.11
  133.9 5.1 collective-permute-done.10
  143.0 5.2 collective-permute-start.13
  149.1 7.9 %collective-permute-done.12 = bf16[128,3072]{1,0:T(8,128)(2,1)S(1)} collective-permute-done((bf16[128,3072]{1,0:T(8,128)(2,1)S(1)}, bf16[128,3072]{1,0:T(8,128)(2,1)S(1)}, u32[]{:S(2)}, u32[]{:S(2)}) %collective-permute-start.12) | collective-permute-done | bytes 786464 | tf_op jit(solution)/shard_map/ppermute | solution.py:19
  162.0 14.1 %collective-permute-done.14 = bf16[128,3072]{1,0:T(8,128)(2,1)S(1)} collective-permute-done((bf16[128,3072]{1,0:T(8,128)(2,1)S(1)}, bf16[128,3072]{1,0:T(8,128)(2,1)S(1)}, u32[]{:S(2)}, u32[]{:S(2)}) %collective-permute-start.14) | collective-permute-done | bytes 786464 | tf_op jit(solution)/shard_map/ppermute | solution.py:19
  177.0 6.4 convolution_convert_fusion.11
  185.4 16.9 %all-to-all-start = ((bf16[4,128,2048]{1,2,0:T(8,128)(2,1)}), bf16[4,128,2048]{1,2,0:T(8,128)(2,1)}, u32[]{:S(2)}, u32[]{:S(2)}) async-start(bf16[4,128,2048]{1,2,0:T(8,128)(2,1)} %broadcast_in_dim.22), calls=%async_computation | async-start | bytes 4194304 | tf_op jit(solution)/shard_map/all_to_all | solution.py:37
  202.9 23.2 %all-to-all-done = bf16[4,128,2048]{1,2,0:T(8,128)(2,1)} async-done(((bf16[4,128,2048]{1,2,0:T(8,128)(2,1)}), bf16[4,128,2048]{1,2,0:T(8,128)(2,1)}, u32[]{:S(2)}, u32[]{:S(2)}) %all-to-all-start) | async-done | bytes 2097184 | tf_op jit(solution)/shard_map/all_to_all | solution.py:37
  226.1 2.9 copy.319
  229.1 14.1 %conditional.7 = (bf16[64,1024]{1,0:T(8,128)(2,1)}, f32[8,64,512]{2,1,0:T(8,128)}, f32[8,64,1]{1,0,2:T(8,128)}, f32[8,64,1]{1,0,2:T(8,128)}, bf16[64,2048]{1,0:T(8,128)(2,1)S(1)}) conditional(s32[]{:T(128)} %convert_element_type.196, () %tuple.76, (bf16[64,1024]{1,0:T(8,128)(2,1)}, bf16[512,2048]{1,0:T(8,128)(2,1)S(1)}, ...), branch_computations={%region_1.2_spmd, %region_2.5_spmd} | conditional | flops 404945920 | bytes 37890116 | solution.py:124
  245.2 4.2 collective-permute-done.15
  251.3 6.8 all-to-all-start.1
  258.1 13.7 %all-to-all-done.1 = bf16[4,64,2048]{2,1,0:T(8,128)(2,1)} async-done(((bf16[4,64,2048]{2,1,0:T(8,128)(2,1)}), bf16[4,64,2048]{2,1,0:T(8,128)(2,1)}, u32[]{:S(2)}, u32[]{:S(2)}) %all-to-all-start.1) | async-done | bytes 1048608 | tf_op jit(solution)/shard_map/all_to_all | solution.py:37
  271.8 4.5 conditional.9
  278.6 5.1 all-to-all-start.2
  283.7 13.7 %all-to-all-done.2 = bf16[4,64,2048]{2,1,0:T(8,128)(2,1)} async-done(((bf16[4,64,2048]{2,1,0:T(8,128)(2,1)}), bf16[4,64,2048]{2,1,0:T(8,128)(2,1)}, u32[]{:S(2)}, u32[]{:S(2)}) %all-to-all-start.2) | async-done | bytes 1048608 | tf_op jit(solution)/shard_map/all_to_all | solution.py:60
  297.4 7.9 %conditional.10 = (bf16[128,2048]{1,0:T(8,128)(2,1)}, bf16[64,2048]{1,0:T(8,128)(2,1)}, f32[2048]{0:T(1024)S(1)}, bf16[2048,3072]{0,1:T(8,128)(2,1)}) conditional(s32[]{:T(128)} %convert_element_type.200, () %tuple.78, (bf16[128,2048]{1,0:T(8,128)(2,1)S(1)}, bf16[128,3072]{0,1:T(8,128)(2,1)}, bf16[4,64,2048]{2,1,0:T(8,128)(2,1)}, ...), branch_computations={%region_13.14_spmd, %region_14.20_spmd} | conditional | flops 4313053184 | bytes 156054880 | solution.py:124
  299.0 6.1 broadcast.200.clone
  306.6 125.6 %collective-permute-done.16 = bf16[64,2048]{1,0:T(8,128)(2,1)S(1)} collective-permute-done((bf16[64,2048]{1,0:T(8,128)(2,1)}, bf16[64,2048]{1,0:T(8,128)(2,1)S(1)}, u32[]{:S(2)}, u32[]{:S(2)}) %collective-permute-start.16) | collective-permute-done | bytes 262176 | tf_op jit(solution)/shard_map/ppermute | solution.py:49
  432.2 16.0 %conditional.11 = (bf16[1024,2048]{1,0:T(8,128)(2,1)}, bf16[64,1024]{1,0:T(8,128)(2,1)}, f32[8,64,1]{1,0,2:T(8,128)}, bf16[64,1024]{1,0:T(8,128)(2,1)S(1)}) conditional(s32[]{:T(128)} %convert_element_type.196, () %tuple.75, (bf16[64,1024]{1,0:T(8,128)(2,1)}, bf16[64,2048]{1,0:T(8,128)(2,1)S(1)}, bf16[1024,2048]{1,0:T(8,128)(2,1)}, ...), branch_computations={%region_20.21_spmd, %region_21.23_spmd} | conditional | flops 674889216 | bytes 41160764 | solution.py:124
  444.0 4.1 convolution_convert_fusion.5
  449.9 4.7 broadcast_select_fusion.1
  455.5 7.4 all_gather.17
  465.8 8.9 %conditional.12 = (bf16[128,2048]{0,1:T(8,128)(2,1)S(1)}) conditional(s32[]{:T(128)} %convert_element_type.196, () %tuple.85, (bf16[256,2048]{1,0:T(8,128)(2,1)}, bf16[128,2048]{1,0:T(8,128)(2,1)S(1)}, f32[24,256,1]{0,2,1:T(1,128)S(1)}) %tuple.183), branch_computations={%region_23.24_spmd, %region_24.25_spmd} | conditional | flops 271843328 | bytes 13754376 | solution.py:124
  474.7 32.4 %conditional.13 = (bf16[2048,3072]{0,1:T(8,128)(2,1)}, bf16[128,2048]{1,0:T(8,128)(2,1)}, f32[2048]{0:T(1024)S(1)}) conditional(s32[]{:T(128)} %convert_element_type.196, () %tuple.74, (bf16[128,2048]{1,0:T(8,128)(2,1)S(1)}, bf16[64,1024]{1,0:T(8,128)(2,1)S(1)}, bf16[128,2048]{0,1:T(8,128)(2,1)S(1)}, f32[128,1]{0,1:T(1,128)}, ...), branch_computations={%region_25.26_spmd, %region_26.0_spmd} | conditional | flops 2721184000 | bytes 65828460 | solution.py:124
  476.4 7.2 fusion.101
  483.6 3.6 fusion.108
  492.5 14.6 %pad_maximum_fusion.5 = bf16[2048,3072]{0,1:T(8,128)(2,1)} fusion(bf16[2048,2048]{0,1:T(8,128)(2,1)S(1)} %convolution_convert_fusion.9, bf16[2048,1024]{0,1:T(8,128)(2,1)S(1)} %convolution_convert_fusion.10), kind=kLoop, calls=%fused_computation.121 | loop fusion | flops 25165824 | bytes 25165824 | tf_op jit(solution)/shard_map/cond/branch_1_fun/concatenate | solution.py:348
  507.1 10.7 %broadcast_select_fusion = bf16[2048,3072]{0,1:T(8,128)(2,1)} fusion(bf16[2048,3072]{0,1:T(8,128)(2,1)} %get-tuple-element.206, bf16[2048,3072]{0,1:T(8,128)(2,1)} %get-tuple-element.450, pred[]{:T(512)S(6)} %eq.19), kind=kLoop, calls=%fused_computation.146 | loop fusion | flops 6291456 | bytes 37748736 | tf_op jit(solution)/shard_map/jit(_where)/select_n | solution.py:362
  520.5 110.1 %reduce-scatter.4.cloned.1.call-done = bf16[2048,768]{0,1:T(8,128)(2,1)} async-done(((bf16[2048,3072]{0,1:T(8,128)(2,1)}), bf16[2048,768]{0,1:T(8,128)(2,1)}) %reduce-scatter.4.cloned.1.call-update) | async-done | bytes 3145744 | tf_op jit(solution)/shard_map/reduce_scatter | solution.py:366
  630.6 3.2 copy.330
  636.3 4.4 pad_maximum_fusion.6
  640.8 4.9 reshape.278
  645.8 76.7 %reduce-scatter.8.cloned.1.call-done = bf16[1024,128]{1,0:T(8,128)(2,1)} async-done(((bf16[16384,128]{1,0:T(8,128)(2,1)}), bf16[1024,128]{1,0:T(8,128)(2,1)}) %reduce-scatter.8.cloned.1.call-update) | async-done | bytes 262160 | tf_op jit(solution)/shard_map/reduce_scatter | solution.py:77
  726.0 8.7 %all-to-all-start.3 = ((f32[64,1,2048]{2,1,0:T(1,128)}), f32[64,1,2048]{2,1,0:T(1,128)S(1)}, u32[]{:S(2)}, u32[]{:S(2)}) async-start(f32[64,1,2048]{2,1,0:T(1,128)} %broadcast_in_dim.29), calls=%async_computation.6 | async-start | bytes 1048576 | tf_op jit(solution)/shard_map/all_to_all | solution.py:37
  736.7 10.2 %all-to-all-done.3 = f32[64,1,2048]{2,1,0:T(1,128)S(1)} async-done(((f32[64,1,2048]{2,1,0:T(1,128)}), f32[64,1,2048]{2,1,0:T(1,128)S(1)}, u32[]{:S(2)}, u32[]{:S(2)}) %all-to-all-start.3) | async-done | bytes 524320 | tf_op jit(solution)/shard_map/all_to_all | solution.py:37
  747.9 4.5 all-gather.10.cloned.1.call-done
  (149 shorter events, 115.4 us)
Async XLA Ops:
  7.2 221.9 %all-gather.8.cloned.1.call-start = ((), (), s32[]{:S(2)}) async-start(), calls=%async_computation.11 | async-start | bytes 4456448 | tf_op jit(solution)/shard_map/all_gather | solution.py:217
  7.2 23.3 %collective-permute-start = (bf16[128,3072]{1,0:T(8,128)(2,1)}, bf16[128,3072]{1,0:T(8,128)(2,1)S(1)}, u32[]{:S(2)}, u32[]{:S(2)}) collective-permute-start(bf16[128,3072]{1,0:T(8,128)(2,1)} %bitcast.212), channel_id=1, source_target_pairs={{0,1},{1,2},{2,3},{3,4},{4,5},{5,6},{6,7},{7,8},{8,9},{9,10},{10,1... | collective-permute-start | bytes 2359304 | tf_op jit(solution)/shard_map/ppermute | solution.py:19
  9.3 22.7 %collective-permute-start.1 = (bf16[128,3072]{1,0:T(8,128)(2,1)}, bf16[128,3072]{1,0:T(8,128)(2,1)S(1)}, u32[]{:S(2)}, u32[]{:S(2)}) collective-permute-start(bf16[128,3072]{1,0:T(8,128)(2,1)} %bitcast.213), channel_id=1, source_target_pairs={{0,15},{1,0},{2,1},{3,2},{4,3},{5,4},{6,5},{7,6},{8,7},{9,8},{10,9... | collective-permute-start | bytes 2359304 | tf_op jit(solution)/shard_map/ppermute | solution.py:22
  30.5 28.9 %copy-start.13 = (bf16[128,3072]{1,0:T(8,128)(2,1)}, bf16[128,3072]{1,0:T(8,128)(2,1)S(1)}, u32[]{:S(2)}) copy-start(bf16[128,3072]{1,0:T(8,128)(2,1)S(1)} %collective-permute-done) | copy-start | bytes 2359300
  30.5 22.8 %collective-permute-start.2 = (bf16[128,3072]{1,0:T(8,128)(2,1)S(1)}, bf16[128,3072]{1,0:T(8,128)(2,1)S(1)}, u32[]{:S(2)}, u32[]{:S(2)}) collective-permute-start(bf16[128,3072]{1,0:T(8,128)(2,1)S(1)} %collective-permute-done), channel_id=1, source_target_pairs={{0,1},{1,2},{2,3},{3,4},{4,5},{5,6},{6,7},{7,8},{8,9},{9,10},{10,1... | collective-permute-start | bytes 2359304 | tf_op jit(solution)/shard_map/ppermute | solution.py:19
  32.0 28.4 %collective-permute-start.3 = (bf16[128,3072]{1,0:T(8,128)(2,1)S(1)}, bf16[128,3072]{1,0:T(8,128)(2,1)}, u32[]{:S(2)}, u32[]{:S(2)}) collective-permute-start(bf16[128,3072]{1,0:T(8,128)(2,1)S(1)} %collective-permute-done.1), channel_id=1, source_target_pairs={{0,15},{1,0},{2,1},{3,2},{4,3},{5,4},{6,5},{7,6},{8,7},{9,8},{10,9... | collective-permute-start | bytes 2359304 | tf_op jit(solution)/shard_map/ppermute | solution.py:22
  53.3 20.7 %collective-permute-start.4 = (bf16[128,3072]{1,0:T(8,128)(2,1)S(1)}, bf16[128,3072]{1,0:T(8,128)(2,1)}, u32[]{:S(2)}, u32[]{:S(2)}) collective-permute-start(bf16[128,3072]{1,0:T(8,128)(2,1)S(1)} %collective-permute-done.2), channel_id=1, source_target_pairs={{0,1},{1,2},{2,3},{3,4},{4,5},{5,6},{6,7},{7,8},{8,9},{9,10},{10,1... | collective-permute-start | bytes 2359304 | tf_op jit(solution)/shard_map/ppermute | solution.py:19
  53.3 244.1 %copy-start.19 = (f32[128,1]{0,1:T(1,128)}, f32[128,1]{0,1:T(1,128)S(1)}, u32[]{:S(2)}) copy-start(f32[128,1]{0,1:T(1,128)S(1)} %get-tuple-element.484) | copy-start | bytes 1540
  53.3 6.1 copy-start.12
  53.3 20.7 %copy-start.2 = (bf16[1,1,128,2048]{3,2,1,0:T(8,128)(2,1)S(1)}, bf16[1,1,128,2048]{3,2,1,0:T(8,128)(2,1)}, u32[]{:S(2)}) copy-start(bf16[1,1,128,2048]{3,2,1,0:T(8,128)(2,1)} %param.25) | copy-start | bytes 1572868
  53.3 20.7 %copy-start.14 = (f32[1,2048]{1,0:T(1,128)S(1)}, f32[1,2048]{1,0:T(1,128)}, u32[]{:S(2)}) copy-start(f32[1,2048]{1,0:T(1,128)} %param.28) | copy-start | bytes 24580
  60.4 18.1 %collective-permute-start.5 = (bf16[128,3072]{1,0:T(8,128)(2,1)}, bf16[128,3072]{1,0:T(8,128)(2,1)}, u32[]{:S(2)}, u32[]{:S(2)}) collective-permute-start(bf16[128,3072]{1,0:T(8,128)(2,1)} %collective-permute-done.3), channel_id=1, source_target_pairs={{0,15},{1,0},{2,1},{3,2},{4,3},{5,4},{6,5},{7,6},{8,7},{9,8},{10,9... | collective-permute-start | bytes 2359304 | tf_op jit(solution)/shard_map/ppermute | solution.py:22
  74.0 27.1 %collective-permute-start.6 = (bf16[128,3072]{1,0:T(8,128)(2,1)}, bf16[128,3072]{1,0:T(8,128)(2,1)}, u32[]{:S(2)}, u32[]{:S(2)}) collective-permute-start(bf16[128,3072]{1,0:T(8,128)(2,1)} %collective-permute-done.4), channel_id=1, source_target_pairs={{0,1},{1,2},{2,3},{3,4},{4,5},{5,6},{6,7},{7,8},{8,9},{9,10},{10,1... | collective-permute-start | bytes 2359304 | tf_op jit(solution)/shard_map/ppermute | solution.py:19
  78.5 33.3 %collective-permute-start.7 = (bf16[128,3072]{1,0:T(8,128)(2,1)}, bf16[128,3072]{1,0:T(8,128)(2,1)S(1)}, u32[]{:S(2)}, u32[]{:S(2)}) collective-permute-start(bf16[128,3072]{1,0:T(8,128)(2,1)} %collective-permute-done.5), channel_id=1, source_target_pairs={{0,15},{1,0},{2,1},{3,2},{4,3},{5,4},{6,5},{7,6},{8,7},{9,8},{10,9... | collective-permute-start | bytes 2359304 | tf_op jit(solution)/shard_map/ppermute | solution.py:22
  101.1 20.9 %collective-permute-start.8 = (bf16[128,3072]{1,0:T(8,128)(2,1)}, bf16[128,3072]{1,0:T(8,128)(2,1)S(1)}, u32[]{:S(2)}, u32[]{:S(2)}) collective-permute-start(bf16[128,3072]{1,0:T(8,128)(2,1)} %collective-permute-done.6), channel_id=1, source_target_pairs={{0,1},{1,2},{2,3},{3,4},{4,5},{5,6},{6,7},{7,8},{8,9},{9,10},{10,1... | collective-permute-start | bytes 2359304 | tf_op jit(solution)/shard_map/ppermute | solution.py:19
  111.8 15.6 %collective-permute-start.9 = (bf16[128,3072]{1,0:T(8,128)(2,1)S(1)}, bf16[128,3072]{1,0:T(8,128)(2,1)S(1)}, u32[]{:S(2)}, u32[]{:S(2)}) collective-permute-start(bf16[128,3072]{1,0:T(8,128)(2,1)S(1)} %collective-permute-done.7), channel_id=1, source_target_pairs={{0,15},{1,0},{2,1},{3,2},{4,3},{5,4},{6,5},{7,6},{8,7},{9,8},{10,9... | collective-permute-start | bytes 2359304 | tf_op jit(solution)/shard_map/ppermute | solution.py:22
  122.1 16.9 %collective-permute-start.10 = (bf16[128,3072]{1,0:T(8,128)(2,1)S(1)}, bf16[128,3072]{1,0:T(8,128)(2,1)S(1)}, u32[]{:S(2)}, u32[]{:S(2)}) collective-permute-start(bf16[128,3072]{1,0:T(8,128)(2,1)S(1)} %collective-permute-done.8), channel_id=1, source_target_pairs={{0,1},{1,2},{2,3},{3,4},{4,5},{5,6},{6,7},{7,8},{8,9},{9,10},{10,1... | collective-permute-start | bytes 2359304 | tf_op jit(solution)/shard_map/ppermute | solution.py:19
  127.4 15.6 %collective-permute-start.11 = (bf16[128,3072]{1,0:T(8,128)(2,1)S(1)}, bf16[128,3072]{1,0:T(8,128)(2,1)S(1)}, u32[]{:S(2)}, u32[]{:S(2)}) collective-permute-start(bf16[128,3072]{1,0:T(8,128)(2,1)S(1)} %collective-permute-done.9), channel_id=1, source_target_pairs={{0,15},{1,0},{2,1},{3,2},{4,3},{5,4},{6,5},{7,6},{8,7},{9,8},{10,9... | collective-permute-start | bytes 2359304 | tf_op jit(solution)/shard_map/ppermute | solution.py:22
  139.0 18.0 %collective-permute-start.12 = (bf16[128,3072]{1,0:T(8,128)(2,1)S(1)}, bf16[128,3072]{1,0:T(8,128)(2,1)S(1)}, u32[]{:S(2)}, u32[]{:S(2)}) collective-permute-start(bf16[128,3072]{1,0:T(8,128)(2,1)S(1)} %collective-permute-done.10), channel_id=1, source_target_pairs={{0,1},{1,2},{2,3},{3,4},{4,5},{5,6},{6,7},{7,8},{8,9},{9,10},{10,1... | collective-permute-start | bytes 2359304 | tf_op jit(solution)/shard_map/ppermute | solution.py:19
  143.0 18.1 %collective-permute-start.13 = (bf16[128,3072]{1,0:T(8,128)(2,1)S(1)}, bf16[128,3072]{1,0:T(8,128)(2,1)S(1)}, u32[]{:S(2)}, u32[]{:S(2)}) collective-permute-start(bf16[128,3072]{1,0:T(8,128)(2,1)S(1)} %collective-permute-done.11), channel_id=1, source_target_pairs={{0,15},{1,0},{2,1},{3,2},{4,3},{5,4},{6,5},{7,6},{8,7},{9,8},{10,9... | collective-permute-start | bytes 2359304 | tf_op jit(solution)/shard_map/ppermute | solution.py:22
  157.0 19.1 %collective-permute-start.14 = (bf16[128,3072]{1,0:T(8,128)(2,1)S(1)}, bf16[128,3072]{1,0:T(8,128)(2,1)S(1)}, u32[]{:S(2)}, u32[]{:S(2)}) collective-permute-start(bf16[128,3072]{1,0:T(8,128)(2,1)S(1)} %collective-permute-done.12), channel_id=1, source_target_pairs={{0,1},{1,2},{2,3},{3,4},{4,5},{5,6},{6,7},{7,8},{8,9},{9,10},{10,1... | collective-permute-start | bytes 2359304 | tf_op jit(solution)/shard_map/ppermute | solution.py:19
  183.4 18.8 %copy-start.3 = (bf16[128,3072]{1,0:T(8,128)(2,1)}, bf16[128,3072]{1,0:T(8,128)(2,1)S(1)}, u32[]{:S(2)}) copy-start(bf16[128,3072]{1,0:T(8,128)(2,1)S(1)} %convolution_convert_fusion.11) | copy-start | bytes 2359300
  183.5 19.4 %copy-start.6 = (bf16[128,2048]{1,0:T(8,128)(2,1)}, bf16[128,2048]{1,0:T(8,128)(2,1)S(1)}, u32[]{:S(2)}) copy-start(bf16[128,2048]{1,0:T(8,128)(2,1)S(1)} %slice.177) | copy-start | bytes 1572868
  185.4 40.7 %all-to-all-start = ((bf16[4,128,2048]{1,2,0:T(8,128)(2,1)}), bf16[4,128,2048]{1,2,0:T(8,128)(2,1)}, u32[]{:S(2)}, u32[]{:S(2)}) async-start(bf16[4,128,2048]{1,2,0:T(8,128)(2,1)} %broadcast_in_dim.22), calls=%async_computation | async-start | bytes 4194304 | tf_op jit(solution)/shard_map/all_to_all | solution.py:37
  233.5 8.0 %copy-start = (bf16[1024,2048]{1,0:T(8,128)(2,1)S(1)}, bf16[1024,2048]{1,0:T(8,128)(2,1)}, u32[]{:S(2)}) copy-start(bf16[1024,2048]{1,0:T(8,128)(2,1)} %get-tuple-element.129) | copy-start | bytes 12582916 | tf_op jit(solution)/shard_map/cond
  243.2 0.7 copy-start.15
  243.9 5.5 collective-permute-start.15
  251.3 20.5 %all-to-all-start.1 = ((bf16[4,64,2048]{2,1,0:T(8,128)(2,1)}), bf16[4,64,2048]{2,1,0:T(8,128)(2,1)}, u32[]{:S(2)}, u32[]{:S(2)}) async-start(bf16[4,64,2048]{2,1,0:T(8,128)(2,1)} %broadcast_in_dim.25), calls=%async_computation.1 | async-start | bytes 2097152 | tf_op jit(solution)/shard_map/all_to_all | solution.py:37
  278.6 18.8 %all-to-all-start.2 = ((bf16[4,64,2048]{2,1,0:T(8,128)(2,1)}), bf16[4,64,2048]{2,1,0:T(8,128)(2,1)}, u32[]{:S(2)}, u32[]{:S(2)}) async-start(bf16[4,64,2048]{2,1,0:T(8,128)(2,1)} %bitcast.190), calls=%async_computation.2 | async-start | bytes 2097152 | tf_op jit(solution)/shard_map/all_to_all | solution.py:60
  283.7 182.1 %all-gather.6.cloned.1.call-start = ((), (), s32[]{:S(2)}) async-start(), calls=%async_computation.7 | async-start | bytes 1310720 | tf_op jit(solution)/shard_map/all_gather | solution.py:67
  305.3 126.9 %copy-start.17 = (f32[2048]{0:T(1024)}, f32[2048]{0:T(1024)S(1)}, u32[]{:S(2)}) copy-start(f32[2048]{0:T(1024)S(1)} %get-tuple-element.211) | copy-start | bytes 24580
  305.3 126.9 %collective-permute-start.16 = (bf16[64,2048]{1,0:T(8,128)(2,1)}, bf16[64,2048]{1,0:T(8,128)(2,1)S(1)}, u32[]{:S(2)}, u32[]{:S(2)}) collective-permute-start(bf16[64,2048]{1,0:T(8,128)(2,1)} %get-tuple-element.197), channel_id=1, source_target_pairs={{64,0},{65,1},{66,2},{67,3},{68,4},{69,5},{70,6},{71,7},{72,8},{73... | collective-permute-start | bytes 786440 | tf_op jit(solution)/shard_map/ppermute | solution.py:49
  435.1 2.8 copy-start.1
  449.9 68.3 %reduce-scatter.6.cloned.1.call-start = ((), (), s32[]{:S(2)}) async-start(), calls=%async_computation.9 | async-start | bytes 5242880 | tf_op jit(solution)/shard_map/reduce_scatter | solution.py:369
  454.6 11.2 %copy-start.7 = (bf16[128,2048]{1,0:T(8,128)(2,1)S(1)}, bf16[128,2048]{1,0:T(8,128)(2,1)}, u32[]{:S(2)}) copy-start(bf16[128,2048]{1,0:T(8,128)(2,1)} %copy-done.6) | copy-start | bytes 1572868
  454.6 175.9 %reduce-scatter.4.cloned.1.call-start = ((), (), s32[]{:S(2)}) async-start(), calls=%async_computation.8 | async-start | bytes 15728640 | tf_op jit(solution)/shard_map/reduce_scatter | solution.py:366
  474.9 0.8 copy-start.8
  483.6 3.6 copy-start.20
  488.9 1.3 copy-start.9
  517.9 204.5 %reduce-scatter.8.cloned.1.call-start = ((), (), s32[]{:S(2)}) async-start(), calls=%async_computation.10 | async-start | bytes 4456448 | tf_op jit(solution)/shard_map/reduce_scatter | solution.py:77
  645.7 79.3 %copy-start.18 = (f32[2048]{0:T(1024)S(1)}, f32[2048]{0:T(1024)}, u32[]{:S(2)}) copy-start(f32[2048]{0:T(1024)} %copy-done.17) | copy-start | bytes 24580
  645.7 106.7 %all-gather.10.cloned.1.call-start = ((), (), s32[]{:S(2)}) async-start(), calls=%async_computation.12 | async-start | bytes 1310720 | tf_op jit(solution)/shard_map/all_gather | solution.py:87
  726.0 20.9 %all-to-all-start.3 = ((f32[64,1,2048]{2,1,0:T(1,128)}), f32[64,1,2048]{2,1,0:T(1,128)S(1)}, u32[]{:S(2)}, u32[]{:S(2)}) async-start(f32[64,1,2048]{2,1,0:T(1,128)} %broadcast_in_dim.29), calls=%async_computation.6 | async-start | bytes 1048576 | tf_op jit(solution)/shard_map/all_to_all | solution.py:37
Sparse Core Ops, SparseCore 0:
  30.6 86.0 all-gather.7
  450.0 15.7 all-gather.5
  468.2 45.7 reduce-scatter.5
  518.0 112.5 reduce-scatter.3
  645.8 76.5 reduce-scatter.7
  725.1 27.2 all-gather.9
